TPU v7x, 128 devices: a whole 4x4x4 slice. The times are simulated.
128 devices in a mesh: fsdp: 32 (over z_lo, x, y), dp: 4 (over z_hi, core).
Axes of the slice: x: 4, y: 4, z: 4 (z_hi: 2, z_lo: 2; z = z_hi * 2 + z_lo), core: 2. Of those that a mesh axis runs over, the one named last changes fastest.
Arguments:
- tokens: bfloat16 [49152, 8192], P(('fsdp', 'dp')), may hold values from -6 to 6
- output_gradient: bfloat16 [49152, 1024], P(('fsdp', 'dp')), may hold values from -6 to 6
- frozen_value_weight: bfloat16 [8192, 1024], P('fsdp'), may hold values from -0.0625 to 0.0625
- adapter_down_maps: bfloat16 [128, 16, 8192], P(('fsdp', 'dp')), may hold values from -0.0625 to 0.0625
- adapter_up_maps: bfloat16 [128, 16, 1024], P(('fsdp', 'dp')), may hold values from -1.5 to 1.5
- block_tenant_ids: int32 [384], P(('fsdp', 'dp')), may hold values from 0 to 127, as said below
- block_live_rows: int32 [384], P(('fsdp', 'dp')), may hold values from 33 to 128, as said below
- tenant_owner_slot: int32 [128], replicated, may hold values from 0 to 127, as said below
Outputs:
- output: bfloat16 [49152, 1024], P(('fsdp', 'dp'))
- token_gradient: bfloat16 [49152, 8192], P(('fsdp', 'dp'))
- grad_down: bfloat16 [128, 16, 8192], P(('fsdp', 'dp'))
- grad_up: bfloat16 [128, 16, 1024], P(('fsdp', 'dp'))
Inputs may be any that keep to these rules, and one draw needn't show every extreme that they name: `block_tenant_ids`: A block held by a device whose index along dp is d names a tenant t with tenant_owner_slot[t] mod (size of dp) = d; tenant_owner_slot is a permutation. `block_live_rows`: the first block of every device is full. `tenant_owner_slot`: each slot is named once.
All inputs are finite; a program needn't handle non-finite values.
Results may differ from a plain program's by a relative error of at most 0.01.
Values may be sent and summed in bfloat16 or wider, within the bound.
A program may use at most 192 MiB of HBM per device.

v0:
```python
import jax
import jax.numpy as jnp
from jax import lax
from jax.sharding import PartitionSpec as P

ADAPTER_SCALE = 2.0


def on_device(
    tokens,
    output_gradient,
    frozen_value_weight,
    adapter_down_maps,
    adapter_up_maps,
    block_tenant_ids,
    block_live_rows,
    tenant_owner_slot,
):
    tok_rows = tokens.shape[0]
    model_width_size = tokens.shape[1]
    value_width_size = output_gradient.shape[1]
    adapter_rank_size = adapter_down_maps.shape[1]
    number_of_blocks = block_tenant_ids.shape[0]
    block_length = tok_rows // number_of_blocks
    groups = lax.axis_size("dp")
    members = lax.axis_size("fsdp")
    tenant_ids = jnp.arange(tenant_owner_slot.shape[0], dtype=jnp.int32)
    slot_ids = jnp.sum(
        jnp.where(block_tenant_ids[:, None] == tenant_ids[None, :], tenant_owner_slot[None, :], 0),
        axis=1,
    )
    member_ids = slot_ids // groups
    live_rows = (jnp.arange(block_length)[None, :] < block_live_rows[:, None]).astype(jnp.float32)
    live_column = live_rows[:, :, None]
    down_all, up_all = (
        lax.all_gather(adapter_down_maps, "fsdp", axis=0, tiled=True),
        lax.all_gather(adapter_up_maps, "fsdp", axis=0, tiled=True),
    )
    onehot = (member_ids[:, None] == jnp.arange(members)[None, :]).astype(jnp.bfloat16)
    down_block = jnp.dot(onehot, down_all.reshape(members, -1), preferred_element_type=jnp.float32)
    down_block = down_block.astype(jnp.bfloat16).reshape(
        number_of_blocks, adapter_rank_size, model_width_size
    )
    up_block = jnp.dot(onehot, up_all.reshape(members, -1), preferred_element_type=jnp.float32)
    up_block = up_block.astype(jnp.bfloat16).reshape(
        number_of_blocks, adapter_rank_size, value_width_size
    )
    token_blocks = tokens.reshape(number_of_blocks, block_length, model_width_size)
    cot_blocks = output_gradient.reshape(number_of_blocks, block_length, value_width_size)
    low_rank_state = (
        jnp.einsum("cvj,coj->cvo", token_blocks, down_block, preferred_element_type=jnp.float32)
        * live_column
    ).astype(jnp.bfloat16)
    low_rank_gradient = (
        ADAPTER_SCALE
        * jnp.einsum("btv,bkv->btk", cot_blocks, up_block, preferred_element_type=jnp.float32)
        * live_column
    ).astype(jnp.bfloat16)
    adapter_output = jnp.einsum(
        "znr,zrm->znm", low_rank_state, up_block, preferred_element_type=jnp.float32
    )
    adapter_backward = jnp.einsum(
        "uio,uof->uif", low_rank_gradient, down_block, preferred_element_type=jnp.float32
    )
    weight_piece = lax.all_gather(frozen_value_weight, "fsdp", axis=0, tiled=True)
    output_total = jnp.dot(tokens, weight_piece, preferred_element_type=jnp.float32)
    backward_piece = lax.dot_general(
        output_gradient, weight_piece, (((1,), (1,)), ((), ())), preferred_element_type=jnp.float32
    )
    output = live_column * (
        output_total.reshape(number_of_blocks, block_length, value_width_size)
        + ADAPTER_SCALE * adapter_output
    )
    output = output.astype(jnp.bfloat16).reshape(tok_rows, value_width_size)
    token_gradient = live_column * (
        backward_piece.reshape(number_of_blocks, block_length, model_width_size) + adapter_backward
    )
    token_gradient = token_gradient.astype(jnp.bfloat16).reshape(tok_rows, model_width_size)
    partial_down = jnp.einsum(
        "vio,vih->voh", low_rank_gradient, token_blocks, preferred_element_type=jnp.float32
    )
    partial_up = ADAPTER_SCALE * jnp.einsum(
        "btk,btv->bkv", low_rank_state, cot_blocks, preferred_element_type=jnp.float32
    )
    member_range = jnp.arange(members, dtype=jnp.int32)
    table_down = jnp.zeros((members, adapter_rank_size, model_width_size), jnp.float32)
    table_up = jnp.zeros((members, adapter_rank_size, value_width_size), jnp.float32)
    for block_num in range(number_of_blocks):
        picked = (member_range == member_ids[block_num]).astype(jnp.float32)[:, None, None]
        table_down = table_down + picked * partial_down[block_num][None]
        table_up = table_up + picked * partial_up[block_num][None]
    term_down = table_down.astype(jnp.bfloat16)
    term_up = table_up.astype(jnp.bfloat16)
    sum_down, sum_up = (
        lax.psum_scatter(
            term_down.astype(jnp.float32).astype(jnp.bfloat16),
            "fsdp",
            scatter_dimension=0,
            tiled=True,
        ).astype(jnp.float32),
        lax.psum_scatter(
            term_up.astype(jnp.float32).astype(jnp.bfloat16),
            "fsdp",
            scatter_dimension=0,
            tiled=True,
        ).astype(jnp.float32),
    )
    return (output, token_gradient, sum_down.astype(jnp.bfloat16), sum_up.astype(jnp.bfloat16))


def solution(mesh):
    placed = (
        P(("fsdp", "dp"), None),
        P(("fsdp", "dp"), None),
        P("fsdp", None),
        P(("fsdp", "dp"), None, None),
        P(("fsdp", "dp"), None, None),
        P(("fsdp", "dp")),
        P(("fsdp", "dp")),
        P(),
    )
    return jax.shard_map(
        on_device,
        mesh=mesh,
        in_specs=placed,
        out_specs=(
            P(("fsdp", "dp"), None),
            P(("fsdp", "dp"), None),
            P(("fsdp", "dp"), None, None),
            P(("fsdp", "dp"), None, None),
        ),
        check_vma=False,
    )
```

profile of v0, /device:TPU:0, one launch (start us, length us, event | category | flops | bytes accessed | tf_op | source)
XLA Modules:
  0.0 875.2 jit_solution(8259146902070135246)
XLA Ops:
  7.2 0.7 all-gather.8.cloned.1.call-update
  8.0 0.7 all-gather.6.cloned.1.call-update
  8.7 0.7 all-gather.4.cloned.1.call-update
  9.4 0.0 reduce-scatter.5.cloned.1.call-start
  9.4 0.9 select_reduce_fusion
  10.3 0.6 fusion.14
  10.9 1.1 compare_convert_fusion.2
  12.0 1.9 compare_convert_fusion
  13.9 0.7 fusion.11
  14.6 0.7 fusion.10
  15.4 147.7 %all-gather.8.cloned.1.call-done = bf16[32,16,1024]{2,1,0:T(8,128)(2,1)} async-done(((bf16[1,16,1024]{2,1,0:T(8,128)(2,1)}), bf16[32,16,1024]{2,1,0:T(8,128)(2,1)}) %all-gather.8.cloned.1.call-update) | async-done | bytes 1048592 | tf_op jit(solution)/shard_map/all_gather | solution.py:37
  163.1 1.8 copy.14
  164.9 0.3 convolution_convert_fusion.1
  165.2 0.3 fusion.1
  165.6 0.6 copy-done.1
  166.2 3.7 fusion.17
  169.9 162.4 %all-gather.6.cloned.1.call-done = bf16[32,16,8192]{2,1,0:T(8,128)(2,1)} async-done(((bf16[1,16,8192]{2,1,0:T(8,128)(2,1)}), bf16[32,16,8192]{2,1,0:T(8,128)(2,1)}) %all-gather.6.cloned.1.call-update) | async-done | bytes 8388624 | tf_op jit(solution)/shard_map/all_gather | solution.py:36
  332.3 11.3 %copy.12 = bf16[4,8,16,8192]{3,1,2,0:T(8,128)(2,1)} copy(bf16[4,8,16,8192]{3,2,1,0:T(8,128)(2,1)} %bitcast.59) | data formatting | bytes 16777216
  343.6 4.6 convolution_convert_fusion
  348.3 4.5 fusion
  352.8 0.2 convolution_multiply_fusion
  353.1 1.5 add_convert_fusion.1
  354.6 0.2 reduce-scatter.3.cloned.1.call-start
  354.8 0.1 slice_bitcast_fusion.2
  354.9 8.1 add_convert_fusion
  363.1 164.9 %all-gather.4.cloned.1.call-done = bf16[8192,1024]{1,0:T(8,128)(2,1)} async-done(((bf16[256,1024]{1,0:T(8,128)(2,1)}), bf16[8192,1024]{1,0:T(8,128)(2,1)}) %all-gather.4.cloned.1.call-update) | async-done | bytes 16777232 | tf_op jit(solution)/shard_map/all_gather | solution.py:65
  528.0 12.2 %fusion.15 = f32[384,1024]{1,0:T(8,128)S(1)} fusion(bf16[384,8192]{1,0:T(8,128)(2,1)} %param.8, bf16[8192,1024]{1,0:T(8,128)(2,1)} %all-gather.4.cloned.1.call-done), kind=kOutput, calls=%fused_computation.41 | convolution fusion | flops 6442450944 | bytes 24641536 | tf_op jit(solution)/shard_map/dot_general | solution.py:66
  540.1 1.3 multiply_convert_fusion.1
  541.4 12.9 %fusion.16 = f32[384,8192]{1,0:T(8,128)} fusion(bf16[384,1024]{1,0:T(8,128)(2,1)S(1)} %copy-done, bf16[8192,1024]{1,0:T(8,128)(2,1)} %all-gather.4.cloned.1.call-done), kind=kOutput, calls=%fused_computation.42 | convolution fusion | flops 6442450944 | bytes 30146560 | tf_op jit(solution)/shard_map/dot_general | solution.py:67
  554.4 9.2 %multiply_convert_fusion = bf16[3,128,8192]{2,1,0:T(8,128)(2,1)} fusion(f32[3,128,8192]{2,1,0:T(8,128)} %bitcast.56, bf16[3,16,128]{2,1,0:T(8,128)(2,1)S(1)} %copy-done.2, f32[3,128]{1,0:T(4,128)S(1)} %fusion.11, bf16[1,3,16,8192]{3,1,2,0:T(4,128)(2,1)S(1)} %bitcast.58), kind=kOutput, calls=%fused_computation.3 | convolution fusion | flops 110100480 | bytes 19674624 | tf_op jit(solution)/shard_map/uio,uof->uif/dot_general | solution.py:62
  563.6 126.7 %reduce-scatter.5.cloned.1.call-done = bf16[1,16,1024]{2,1,0:T(8,128)(2,1)} async-done(((bf16[32,16,1024]{2,1,0:T(8,128)(2,1)}), bf16[1,16,1024]{2,1,0:T(8,128)(2,1)}) %reduce-scatter.5.cloned.1.call-update) | async-done | bytes 32784 | tf_op jit(solution)/shard_map/reduce_scatter | solution.py:101
  690.3 178.4 %reduce-scatter.3.cloned.1.call-done = bf16[1,16,8192]{2,1,0:T(8,128)(2,1)} async-done(((bf16[32,16,8192]{2,1,0:T(8,128)(2,1)}), bf16[1,16,8192]{2,1,0:T(8,128)(2,1)}) %reduce-scatter.3.cloned.1.call-update) | async-done | bytes 262160 | tf_op jit(solution)/shard_map/reduce_scatter | solution.py:95
  (18 shorter events, 0.2 us)
Async XLA Ops:
  7.2 158.1 %copy-start = (bf16[384,1024]{1,0:T(8,128)(2,1)S(1)}, bf16[384,1024]{1,0:T(8,128)(2,1)}, u32[]{:S(2)}) copy-start(bf16[384,1024]{1,0:T(8,128)(2,1)} %param.9) | copy-start | bytes 2359300
  7.2 155.9 %all-gather.8.cloned.1.call-start = ((), (), s32[]{:S(2)}) async-start(), calls=%async_computation.4 | async-start | bytes 1081344 | tf_op jit(solution)/shard_map/all_gather | solution.py:37
  7.9 324.4 %all-gather.6.cloned.1.call-start = ((), (), s32[]{:S(2)}) async-start(), calls=%async_computation.3 | async-start | bytes 8650752 | tf_op jit(solution)/shard_map/all_gather | solution.py:36
  8.7 519.3 %all-gather.4.cloned.1.call-start = ((), (), s32[]{:S(2)}) async-start(), calls=%async_computation.2 | async-start | bytes 17301504 | tf_op jit(solution)/shard_map/all_gather | solution.py:65
  9.4 680.9 %reduce-scatter.5.cloned.1.call-start = ((), (), s32[]{:S(2)}) async-start(), calls=%async_computation.6 | async-start | bytes 1081344 | tf_op jit(solution)/shard_map/reduce_scatter | solution.py:101
  165.6 0.6 copy-start.1
  348.2 4.8 copy-start.3
  348.2 4.8 copy-start.4
  348.3 4.8 copy-start.5
  354.6 514.1 %reduce-scatter.3.cloned.1.call-start = ((), (), s32[]{:S(2)}) async-start(), calls=%async_computation.5 | async-start | bytes 8650752 | tf_op jit(solution)/shard_map/reduce_scatter | solution.py:95
  541.4 12.9 %copy-start.2 = (bf16[3,16,128]{2,1,0:T(8,128)(2,1)S(1)}, bf16[3,16,128]{2,1,0:T(8,128)(2,1)}, u32[]{:S(2)}) copy-start(bf16[3,16,128]{2,1,0:T(8,128)(2,1)} %copy-done.1) | copy-start | bytes 36868
Sparse Core Ops, SparseCore 0:
  9.7 153.3 all-gather.7
  164.7 167.5 all-gather.5
  333.9 194.0 all-gather.3
  530.8 159.4 reduce-scatter.4
  693.2 175.3 reduce-scatter.2
where the time goes:
time: 876 us; the launch traced here: 875 us
  waiting for transfers between devices  782 us (89%)
  matrix products  49.4 us (6%)
  other arithmetic  14.9 us (2%)
  local copies, waits for them, and re-layouts  14.4 us (2%)
  between operations  13.9 us (2%)
    reduce_scatter x1, waiting for transfers between devices, on_device(): lax.psum_scatter(term_down.astype(jnp.float32).astype(jnp.bfloat16), 'fsd...  178 us
    all_gather x1, waiting for transfers between devices, on_device(): lax.all_gather(frozen_value_weight, 'fsdp', axis=0, tiled=True)  165 us
    all_gather x1, waiting for transfers between devices, on_device(): lax.all_gather(adapter_down_maps, 'fsdp', axis=0, tiled=True)  162 us
    all_gather x1, waiting for transfers between devices, on_device(): lax.all_gather(adapter_up_maps, 'fsdp', axis=0, tiled=True)  148 us
    reduce_scatter x1, waiting for transfers between devices, on_device(): lax.psum_scatter(term_up.astype(jnp.float32).astype(jnp.bfloat16), 'fsdp'...  127 us
  transfers between devices with their start and end apart: 5, of which 5 were waited for; matrix products, arithmetic and copies ran while one was open for 9% of the time, Pallas kernels for 0%

commit v1 on v0

v1 whole, which is shorter than its diff:
```python
import jax
import jax.numpy as jnp
from jax import lax
from jax.experimental import pallas as pl
from jax.experimental.pallas import tpu as pltpu
from jax.sharding import PartitionSpec as P

ADAPTER_SCALE = 2.0
MESH = pl.DeviceIdType.MESH
F32 = jnp.float32
BF16 = jnp.bfloat16
STEP = 1024
NSEM = 96


def mult(index, of):
    return pl.multiple_of(index, of)


def kernel(
    tok_h, cot_h, w_h, down_h, up_h, ids_s, live_s, owner_v,
    out_h, tg_h, gd_h, gu_h,
    tok, cot, wbuf, src, sel, r1, r2, fin, part, tab, t1, t2, t3, zs, gout,
    acc, xb, db, tgb, outb, meta, smat, lg, low, ls, ts, ss, rs,
):
    rows, model = tok_h.shape
    value = cot_h.shape[1]
    rank = down_h.shape[1]
    nblk = ids_s.shape[0]
    block = rows // nblk
    width = model + value
    picks = nblk * rank
    half = w_h.shape[0] // 2

    f_me = lax.axis_index("fsdp")
    d_me = lax.axis_index("dp")
    zl = f_me // 16
    x = f_me // 4 % 4
    y = f_me % 4
    zh = d_me // 2
    c = d_me % 2
    p = y * (1 - c) + x * c
    q = x * (1 - c) + y * c
    sp = 1 + 3 * c
    sq = 4 - 3 * c
    p_r, p_l, p_o = (p + 1) % 4, (p + 3) % 4, (p + 2) % 4

    def device(zl_, p_, q_):
        return (zl_ * 16 + p_ * sp + q_ * sq, d_me)

    to_z = device(1 - zl, p, q)
    to_pr, to_pl = device(zl, p_r, q), device(zl, p_l, q)
    to_qr, to_ql = device(zl, p, (q + 1) % 4), device(zl, p, (q + 3) % 4)
    to_qo = device(zl, p, (q + 2) % 4)
    to_c = (f_me, zh * 2 + 1 - c)

    count = [0]

    def remote(source, target, where):
        i = count[0]
        count[0] += 1
        return pltpu.make_async_remote_copy(
            src_ref=source, dst_ref=target, send_sem=ss.at[i], recv_sem=rs.at[i],
            device_id=where, device_id_type=MESH,
        )

    def start(copies):
        for copy in copies:
            copy.start()

    def recv(copies):
        for copy in copies:
            copy.wait_recv()

    lc_up = pltpu.make_async_copy(up_h.at[0], src.at[zl, p, :, pl.ds(0, value)], ls.at[0])
    lc_down = pltpu.make_async_copy(down_h.at[0], src.at[zl, p, :, pl.ds(value, model)], ls.at[1])
    lc_cot = pltpu.make_async_copy(cot_h, cot, ls.at[2])
    lc_tok = pltpu.make_async_copy(tok_h, tok, ls.at[3])
    w_own = w_h.at[pl.ds(mult(c * half, half), half)]
    lc_w = pltpu.make_async_copy(w_own, wbuf.at[0, 0, zl * 4 + p], ls.at[4])
    start([lc_up, lc_cot, lc_down, lc_w, lc_tok])

    lane = lax.broadcasted_iota(jnp.int32, (8, 128), 1)
    subl = lax.broadcasted_iota(jnp.int32, (8, 128), 0)
    owners = owner_v[...].astype(F32)
    lane1 = lax.broadcasted_iota(jnp.int32, (1, 128), 1)
    mrow = jnp.zeros((8, 128), F32)
    for b in range(nblk):
        slot = jnp.sum(jnp.where(lane1 == ids_s[b], owners, 0.0), axis=1, keepdims=True)
        mrow = jnp.where(subl == b, slot, mrow)
    meta[0] = mrow

    barrier = pltpu.get_barrier_semaphore()
    partners = (to_z, to_pr, to_pl, to_qr, to_ql, to_qo, to_c)
    for where in partners:
        pl.semaphore_signal(barrier, inc=1, device_id=where, device_id_type=MESH)
    pl.semaphore_wait(barrier, len(partners))

    def gather(own, at):
        z = [remote(own, at(zl, p), to_z)]
        p1o = [remote(own, at(zl, p), to_pr), remote(own, at(zl, p), to_pl)]
        theirs = at(1 - zl, p)
        p1z = [remote(theirs, theirs, to_pr), remote(theirs, theirs, to_pl)]
        p2 = [
            remote(at(0, p_l), at(0, p_l), to_pr),
            remote(at(1, p_r), at(1, p_r), to_pl),
        ]
        return z, p1o, p1z, p2

    def adapter_at(first, size):
        return lambda zl_, p_: src.at[zl_, p_, :, pl.ds(first, size)]

    u_z, u_p1o, u_p1z, u_p2 = gather(up_h.at[0], adapter_at(0, value))
    d_z, d_p1o, d_p1z, d_p2 = gather(down_h.at[0], adapter_at(value, model))
    w_z, w_p1o, w_p1z, w_p2 = gather(w_own, lambda zl_, p_: wbuf.at[0, 0, zl_ * 4 + p_])
    m_q = [
        remote(meta.at[0], meta.at[3], to_qr),
        remote(meta.at[0], meta.at[1], to_ql),
        remote(meta.at[0], meta.at[2], to_qo),
    ]

    def scatter_q(first, size):
        h = size // 2
        h0 = first // 2
        q1 = [
            remote(sel.at[2, :, pl.ds(first, h)], r1.at[0, :, pl.ds(h0, h)], to_qr),
            remote(sel.at[2, :, pl.ds(first + h, h)], r1.at[1, :, pl.ds(h0, h)], to_ql),
        ]
        whole = pl.ds(first, size)
        q2 = [
            remote(sel.at[1, :, whole], r2.at[0, :, whole], to_qr),
            remote(sel.at[3, :, whole], r2.at[1, :, whole], to_ql),
        ]
        return q1, q2

    u_q1, u_q2 = scatter_q(0, value)
    d_q1, d_q2 = scatter_q(value, model)

    def grads(first, size):
        h = size // 2
        whole = pl.ds(first, size)
        q1 = [
            remote(part.at[0, :, whole], part.at[3, :, whole], to_qr),
            remote(part.at[0, :, whole], part.at[1, :, whole], to_ql),
        ]
        lo, hi = pl.ds(first, h), pl.ds(first + h, h)
        q2 = [
            remote(part.at[3, :, lo], part.at[2, :, lo], to_qr),
            remote(part.at[1, :, hi], part.at[2, :, hi], to_ql),
        ]
        p1 = [
            remote(tab.at[0, p_o, :, whole], t1.at[0, :, whole], to_pr),
            remote(tab.at[1, p_o, :, whole], t1.at[1, :, whole], to_pl),
        ]
        p2 = [
            remote(tab.at[:, p_r, :, whole], t2.at[0, :, :, whole], to_pr),
            remote(tab.at[:, p_l, :, whole], t2.at[1, :, :, whole], to_pl),
        ]
        z = [remote(zs.at[:, whole], t3.at[:, whole], to_z)]
        return q1, q2, p1, p2, z

    gd = grads(value, model)
    gu = grads(0, value)

    def w_part(dq, zl_):
        return wbuf.at[0, dq, pl.ds(zl_ * 4, 4)]

    w_q1 = [
        remote(w_part(0, 0), w_part(3, 0), to_qr),
        remote(w_part(0, 1), w_part(1, 1), to_ql),
        remote(w_part(0, 1), w_part(3, 1), to_qr),
        remote(w_part(0, 0), w_part(1, 0), to_ql),
    ]
    w_q2 = [
        remote(w_part(3, 0), w_part(2, 0), to_qr),
        remote(w_part(1, 1), w_part(2, 1), to_ql),
    ]
    w_c = [remote(wbuf.at[0, dq], wbuf.at[1, dq], to_c) for dq in range(4)]

    start(u_z + u_p1o + m_q + d_z + d_p1o + w_z + w_p1o)

    def columns(first, j, step=STEP):
        return pl.ds(mult(first + j * step, 128), step)

    def loop(size, body, step=STEP):
        if size <= step:
            body(0, size)
        else:
            def run(j, carry):
                body(j, step)
                return carry
            lax.fori_loop(0, size // step, run, 0)

    def build_selection():
        lanes = lax.broadcasted_iota(jnp.int32, (1, 128), 1)
        j = lanes // 16
        target = (((j // 4) * 16 + (j % 4) * sp + q * sq) * 4 + d_me).astype(F32)
        same = lax.broadcasted_iota(jnp.int32, (16, 128), 0) == (
            lax.broadcasted_iota(jnp.int32, (16, 128), 1) % 16
        )
        for dq in range(4):
            for b in range(nblk):
                hit = jnp.logical_and(same, meta[dq, b : b + 1, :] == target)
                r0 = (dq * nblk + b) * rank
                smat[r0 : r0 + rank, :] = jnp.where(hit, 1.0, 0.0).astype(BF16)

    def select(first, size):
        def one(j, step):
            cols = columns(first, j, step)
            held = src[:, :, :, cols].reshape(8 * rank, step)
            picked = jnp.dot(smat[...], held, preferred_element_type=F32)
            sel[:, :, cols] = picked.astype(BF16).reshape(4, picks, step)
        loop(size, one)

    def add_halves(first, size):
        h = size // 2
        h0 = first // 2

        def one(j, step):
            from_l, from_r = columns(first, j, step), columns(first + h, j, step)
            got = columns(h0, j, step)
            sel[1, :, from_l] = sel[1, :, from_l] + r1[0, :, got]
            sel[3, :, from_r] = sel[3, :, from_r] + r1[1, :, got]
        loop(h, one)

    def finish_selection(first, size):
        def one(j, step):
            cols = columns(first, j, step)
            fin[:, cols] = sel[0, :, cols] + r2[0, :, cols] + r2[1, :, cols]
        loop(size, one)

    def build_table(first, size):
        def one(j, step):
            cols = columns(first, j, step)
            held = part[:, :, cols].reshape(4 * picks, step)
            total = lax.dot_general(
                smat[...], held, (((0,), (0,)), ((), ())), preferred_element_type=F32
            )
            tab[:, :, :, cols] = total.astype(BF16).reshape(2, 4, rank, step)
        loop(size, one)

    def add_table(first, size):
        def one(j, step):
            cols = columns(first, j, step)
            a = tab[0, p_r, :, cols].astype(F32) + t1[0, :, cols].astype(F32)
            tab[0, p_r, :, cols] = a.astype(BF16)
            a = tab[1, p_l, :, cols].astype(F32) + t1[1, :, cols].astype(F32)
            tab[1, p_l, :, cols] = a.astype(BF16)
        loop(size, one)

    def sum_three(zl_, cols):
        return (
            tab[zl_, p, :, cols].astype(F32)
            + t2[0, zl_, :, cols].astype(F32)
            + t2[1, zl_, :, cols].astype(F32)
        )

    def send_table(first, size):
        def one(j, step):
            cols = columns(first, j, step)
            zs[:, cols] = sum_three(1 - zl, cols).astype(BF16)
        loop(size, one)

    def finish_table(first, size):
        def one(j, step):
            cols = columns(first, j, step)
            gout[:, cols] = (sum_three(zl, cols) + t3[:, cols].astype(F32)).astype(BF16)
        loop(size, one)

    def live_mask(shape):
        r = lax.broadcasted_iota(jnp.int32, shape, 0)
        limit = jnp.zeros(shape, jnp.int32)
        for b in range(nblk):
            limit = jnp.where(r // block == b, live_s[b] + b * block, limit)
        return r < limit

    def block_mask():
        r = lax.broadcasted_iota(jnp.int32, (rows, picks), 0)
        k = lax.broadcasted_iota(jnp.int32, (rows, picks), 1)
        return jnp.logical_and(r // block == k // rank, live_mask((rows, picks)))

    def batch(g, dq, t, wait):
        spg = sp + g * (sq - sp)
        sqg = sq + g * (sp - sq)
        qg = q + g * (p - q)
        hg = c + g * (1 - 2 * c)
        slot = t % 2

        def place(i):
            f = (i // 4) * 16 + (i % 4) * spg + ((qg + dq) % 4) * sqg
            return mult(f * (2 * half) + hg * half, half)

        def take(i, carry):
            at = pl.ds(mult(i * half, half), half)
            xb[:, at] = tok[:, pl.ds(place(i), half)]
            db[:, at] = fin[:, pl.ds(mult(value + place(i), half), half)]
            return carry
        lax.fori_loop(0, 8, take, 0)

        def forward(n, carry):
            cols = pl.ds(mult(n * 256, 256), 256)
            w = wbuf[g, dq, :, :, cols].reshape(8 * half, 256)
            acc[:, cols] += jnp.dot(xb[...], w, preferred_element_type=F32)
            return carry
        lax.fori_loop(0, value // 256, forward, 0)

        def out_copy(i):
            return pltpu.make_async_copy(
                tgb.at[slot, :, pl.ds(mult(i * half, half), half)],
                tg_h.at[:, pl.ds(place(i), half)],
                ts.at[slot, i],
            )

        if wait:
            def settle(i, carry):
                out_copy(i).wait()
                return carry
            lax.fori_loop(0, 8, settle, 0)

        def backward(m, carry):
            w = wbuf[g, dq, pl.ds(m * 2, 2), :, :].reshape(2 * half, value)
            at = pl.ds(mult(m * 2 * half, 2 * half), 2 * half)
            got = lax.dot_general(
                cot[...], w, (((1,), (1,)), ((), ())), preferred_element_type=F32
            )
            got = got + jnp.dot(lg[...], db[:, at], preferred_element_type=F32)
            tgb[slot, :, at] = got.astype(BF16)
            return carry
        lax.fori_loop(0, 4, backward, 0)

        def send_out(i, carry):
            out_copy(i).start()
            return carry
        lax.fori_loop(0, 8, send_out, 0)

    U = (0, value)
    D = (value, model)

    recv(u_z)
    start(u_p1z)
    recv(u_p1o + u_p1z)
    start(u_p2)
    recv(d_z)
    start(d_p1z)
    recv(m_q)
    build_selection()
    lc_up.wait()
    recv(u_p2)
    select(*U)
    start(u_q1)
    recv(w_z)
    start(w_p1z)
    recv(u_q1)
    add_halves(*U)
    start(u_q2)
    recv(d_p1o + d_p1z)
    start(d_p2)
    lc_cot.wait()
    cot[...] = jnp.where(live_mask((rows, value)), cot[...].astype(F32), 0.0).astype(BF16)
    recv(u_q2)
    finish_selection(*U)

    back = lax.dot_general(
        cot[...], fin[:, pl.ds(0, value)], (((1,), (1,)), ((), ())), preferred_element_type=F32
    )
    lg[...] = jnp.where(block_mask(), ADAPTER_SCALE * back, 0.0).astype(BF16)
    lc_tok.wait()

    def down_part(j, step):
        got = lax.dot_general(
            lg[...], tok[:, columns(0, j, step)], (((0,), (0,)), ((), ())),
            preferred_element_type=F32,
        )
        part[0, :, columns(value, j, step)] = got.astype(BF16)
    loop(model, down_part)
    start(gd[0])

    lc_down.wait()
    recv(d_p2)
    select(*D)
    start(d_q1)
    recv(w_p1o + w_p1z)
    start(w_p2)
    lc_w.wait()
    recv(w_p2)
    start(w_q1)
    start([w_c[0]])
    recv(gd[0])
    start(gd[1])
    recv(d_q1)
    add_halves(*D)
    start(d_q2)
    recv(gd[1])
    build_table(*D)
    start(gd[2])
    recv(d_q2)
    finish_selection(*D)

    def low_part(j, total):
        return total + lax.dot_general(
            tok[:, columns(0, j)], fin[:, columns(value, j)], (((1,), (1,)), ((), ())),
            preferred_element_type=F32,
        )
    total = lax.fori_loop(0, model // STEP, low_part, jnp.zeros((rows, picks), F32))
    low[...] = jnp.where(block_mask(), total, 0.0).astype(BF16)
    up_part = lax.dot_general(
        low[...], cot[...], (((0,), (0,)), ((), ())), preferred_element_type=F32
    )
    part[0, :, pl.ds(0, value)] = (ADAPTER_SCALE * up_part).astype(BF16)
    start(gu[0])
    acc[...] = ADAPTER_SCALE * jnp.dot(
        low[...], fin[:, pl.ds(0, value)], preferred_element_type=F32
    )
    recv(gd[2])
    add_table(*D)
    start(gd[3])
    recv(gu[0])
    start(gu[1])
    recv([w_c[0]])

    def first_batches(i, carry):
        batch(i, 0, i, False)
        return carry
    lax.fori_loop(0, 2, first_batches, 0)
    recv(gd[3])
    send_table(*D)
    start(gd[4])
    recv(gu[1])
    build_table(*U)
    start(gu[2])
    recv([w_q1[0], w_q1[1]])
    start(w_q2)
    recv(gu[2])
    add_table(*U)
    start(gu[3])
    recv([w_q1[2], w_q1[3]])
    start([w_c[1], w_c[3]])
    recv(gd[4])
    finish_table(*D)
    o_gd = pltpu.make_async_copy(gout.at[:, pl.ds(value, model)], gd_h.at[0], ls.at[5])
    o_gd.start()
    recv(gu[3])
    send_table(*U)
    start(gu[4])
    recv([w_c[1], w_c[3]])

    def middle_batches(i, carry):
        batch(i // 2, 1 + 2 * (i % 2), i + 2, True)
        return carry
    lax.fori_loop(0, 4, middle_batches, 0)
    recv(gu[4])
    finish_table(*U)
    o_gu = pltpu.make_async_copy(gout.at[:, pl.ds(0, value)], gu_h.at[0], ls.at[6])
    o_gu.start()
    recv(w_q2)
    start([w_c[2]])
    recv([w_c[2]])

    def last_batches(i, carry):
        batch(i, 2, i + 6, True)
        return carry
    lax.fori_loop(0, 2, last_batches, 0)
    outb[...] = jnp.where(live_mask((rows, value)), acc[...], 0.0).astype(BF16)
    o_out = pltpu.make_async_copy(outb, out_h, ls.at[7])
    o_out.start()

    sent = u_z + u_p1o + u_p1z + u_p2 + d_z + d_p1o + d_p1z + d_p2 + w_z + w_p1o + w_p1z + w_p2
    sent = sent + m_q + u_q1 + u_q2 + d_q1 + d_q2 + w_q1 + w_q2 + w_c
    for group in gd + gu:
        sent = sent + group
    for copy in sent:
        copy.wait_send()
    o_gd.wait()
    o_gu.wait()
    o_out.wait()
    for slot in range(2):
        for i in range(8):
            pltpu.make_async_copy(
                tgb.at[slot, :, pl.ds(i * half, half)],
                tg_h.at[:, pl.ds(i * half, half)],
                ts.at[slot, i],
            ).wait()


def on_device(
    tokens,
    output_gradient,
    frozen_value_weight,
    adapter_down_maps,
    adapter_up_maps,
    block_tenant_ids,
    block_live_rows,
    tenant_owner_slot,
):
    rows, model = tokens.shape
    value = output_gradient.shape[1]
    rank = adapter_down_maps.shape[1]
    nblk = block_tenant_ids.shape[0]
    picks = nblk * rank
    width = model + value
    half = frozen_value_weight.shape[0] // 2
    hbm = pl.BlockSpec(memory_space=pl.ANY)
    smem = pl.BlockSpec(memory_space=pltpu.SMEM)
    vmem = pl.BlockSpec(memory_space=pltpu.VMEM)
    flops = 4 * rows * model * value
    return pl.pallas_call(
        kernel,
        out_shape=(
            jax.ShapeDtypeStruct((rows, value), BF16),
            jax.ShapeDtypeStruct((rows, model), BF16),
            jax.ShapeDtypeStruct((1, rank, model), BF16),
            jax.ShapeDtypeStruct((1, rank, value), BF16),
        ),
        in_specs=[hbm] * 5 + [smem, smem, vmem],
        out_specs=(hbm, hbm, hbm, hbm),
        scratch_shapes=[
            pltpu.VMEM((rows, model), BF16),
            pltpu.VMEM((rows, value), BF16),
            pltpu.VMEM((2, 4, 8, half, value), BF16),
            pltpu.VMEM((2, 4, rank, width), BF16),
            pltpu.VMEM((4, picks, width), BF16),
            pltpu.VMEM((2, picks, width // 2), BF16),
            pltpu.VMEM((2, picks, width), BF16),
            pltpu.VMEM((picks, width), BF16),
            pltpu.VMEM((4, picks, width), BF16),
            pltpu.VMEM((2, 4, rank, width), BF16),
            pltpu.VMEM((2, rank, width), BF16),
            pltpu.VMEM((2, 2, rank, width), BF16),
            pltpu.VMEM((rank, width), BF16),
            pltpu.VMEM((rank, width), BF16),
            pltpu.VMEM((rank, width), BF16),
            pltpu.VMEM((rows, value), F32),
            pltpu.VMEM((rows, 8 * half), BF16),
            pltpu.VMEM((picks, 8 * half), BF16),
            pltpu.VMEM((2, rows, 8 * half), BF16),
            pltpu.VMEM((rows, value), BF16),
            pltpu.VMEM((4, 8, 128), F32),
            pltpu.VMEM((4 * picks, 8 * rank), BF16),
            pltpu.VMEM((rows, picks), BF16),
            pltpu.VMEM((rows, picks), BF16),
            pltpu.SemaphoreType.DMA((8,)),
            pltpu.SemaphoreType.DMA((2, 8)),
            pltpu.SemaphoreType.DMA((NSEM,)),
            pltpu.SemaphoreType.DMA((NSEM,)),
        ],
        compiler_params=pltpu.CompilerParams(
            collective_id=0, has_side_effects=True, vmem_limit_bytes=58 * 2**20
        ),
        cost_estimate=pl.CostEstimate(
            flops=flops, bytes_accessed=4 * rows * model, transcendentals=0
        ),
    )(
        tokens,
        output_gradient,
        frozen_value_weight,
        adapter_down_maps,
        adapter_up_maps,
        block_tenant_ids,
        block_live_rows,
        tenant_owner_slot.reshape(1, -1),
    )


def solution(mesh):
    placed = (
        P(("fsdp", "dp"), None),
        P(("fsdp", "dp"), None),
        P("fsdp", None),
        P(("fsdp", "dp"), None, None),
        P(("fsdp", "dp"), None, None),
        P(("fsdp", "dp")),
        P(("fsdp", "dp")),
        P(),
    )
    return jax.shard_map(
        on_device,
        mesh=mesh,
        in_specs=placed,
        out_specs=(
            P(("fsdp", "dp"), None),
            P(("fsdp", "dp"), None),
            P(("fsdp", "dp"), None, None),
            P(("fsdp", "dp"), None, None),
        ),
        check_vma=False,
    )
```

time: 876 us -> 153 us (0.17)
  waiting for transfers between devices: 782 us -> 0 us
  Pallas kernels: 0 us -> 142 us
  matrix products: 49.4 us -> 0 us
  other arithmetic: 14.9 us -> 0 us
  between operations: 13.9 us -> 0.65 us
    all_gather x3 -> x0, waiting for transfers between devices: 475 us -> none  [the longest x1 165 us: on_device(): lax.all_gather(frozen_value_weight, 'fsdp', axis=0, tiled=True)]
    reduce_scatter x2 -> x0, waiting for transfers between devices: 305 us -> none  [the longest x1 178 us: on_device(): lax.psum_scatter(term_down.astype(jnp.float32).astype(jnp.bfloat16), 'fsd...]
    pallas_call x0 -> x1, Pallas kernels: none -> 142 us  [on_device(): pl.pallas_call(kernel, out_shape=(jax.ShapeDtypeStruct((rows, value), BF1...]
    dot_general x10 -> x0, matrix products: 49.4 us -> none  [the longest x1 12.9 us: on_device(): lax.dot_general(output_gradient, weight_piece, (((1,), (1,)), ((), ())),...]
    convert_element_type x5 -> x0, other arithmetic: 13.3 us -> none  [the longest x1 8.11 us: on_device(): term_down = table_down.astype(jnp.bfloat16)]
  transfers between devices with their start and end apart: 5 -> 0, of which waited for: 5 -> 0; matrix products, arithmetic and copies ran while one was open for 9% -> 0% of each run, Pallas kernels for 0% -> 0%
where the time goes in v1:
time: 153 us
  Pallas kernels  142 us (93%)
  local copies, waits for them, and re-layouts  9.63 us (6%)
    pallas_call x1, Pallas kernels, on_device(): pl.pallas_call(kernel, out_shape=(jax.ShapeDtypeStruct((rows, value), BF1...  142 us
    unnamed x8, local copies, waits for them, and re-layouts  9.63 us

profile of v1, /device:TPU:0, one launch (start us, length us, event | category | flops | bytes accessed | tf_op | source)
XLA Modules:
  0.0 152.5 jit_solution(10368644479260807665)
XLA Ops:
  0.6 142.2 %shard_map.111 = (bf16[384,1024]{1,0:T(8,128)(2,1)}, bf16[384,8192]{1,0:T(8,128)(2,1)}, bf16[1,16,8192]{2,1,0:T(8,128)(2,1)}, bf16[1,16,1024]{2,1,0:T(8,128)(2,1)}) custom-call(bf16[384,8192]{1,0:T(8,128)(2,1)} %tok_h.1, bf16[384,1024]{1,0:T(8,128)(2,1)} %cot_h.1, bf16[256,1024]{1,0:T(8,128)(2,1)} %w_h.1, bf16[1,16,8192]{2,1,0:T(8,128)(2,1)} %down_h.1, ...), custom_call_target="tpu_custom_call" | custom-call | flops 12884901888 | bytes 12582912 | tf_op jit(solution)/shard_map/pallas_call | solution.py:506
  142.9 2.1 %copy.16 = bf16[384,1024]{1,0:T(8,128)(2,1)} copy(bf16[384,1024]{1,0:T(8,128)(2,1)} %get-tuple-element.8) | data formatting | bytes 1572864
  145.0 0.0 copy-start
  145.0 0.0 copy-start.1
  145.0 6.2 %copy.17 = bf16[384,8192]{1,0:T(8,128)(2,1)} copy(bf16[384,8192]{1,0:T(8,128)(2,1)} %get-tuple-element.9) | data formatting | bytes 12582912
  151.2 0.0 copy-done
  151.2 0.7 copy.18
  151.9 0.0 copy-done.1
  151.9 0.6 copy.19
Async XLA Ops:
  145.0 6.2 %copy-start = (bf16[1,16,8192]{2,1,0:T(8,128)(2,1)S(1)}, bf16[1,16,8192]{2,1,0:T(8,128)(2,1)}, u32[]{:S(2)}) copy-start(bf16[1,16,8192]{2,1,0:T(8,128)(2,1)} %get-tuple-element.10) | copy-start | bytes 786436
  145.0 6.9 %copy-start.1 = (bf16[1,16,1024]{2,1,0:T(8,128)(2,1)S(1)}, bf16[1,16,1024]{2,1,0:T(8,128)(2,1)}, u32[]{:S(2)}) copy-start(bf16[1,16,1024]{2,1,0:T(8,128)(2,1)} %get-tuple-element.11) | copy-start | bytes 98308

commit v2 on v1

--- a/solution.py
+++ b/solution.py
@@ -10,7 +10,13 @@
 F32 = jnp.float32
 BF16 = jnp.bfloat16
 STEP = 1024
-NSEM = 96
+NSEM = 128
+PARTS = 2
+ORDER = (
+    "U S D0 D1", "W W M U", "D0 W D1 U", "W D0 D1 S", "U W W D0", "D1 U C W",
+    "W W D0 D1", "U LG G0 G1", "D0 D1 L G0", "GU L C B", "W W B G1", "B G0 GU G1",
+    "B G0 GU G1", "B C B G0", "GU B G1 GU", "B G0 G1 GU",
+)
 
 
 def mult(index, of):
@@ -49,6 +55,12 @@
         return (zl_ * 16 + p_ * sp + q_ * sq, d_me)
 
     to_z = device(1 - zl, p, q)
+    z = zh * 2 + zl
+
+    def along_z(z_):
+        return (z_ % 2 * 16 + f_me % 16, z_ // 2 * 2 + c)
+
+    to_zu, to_zd = along_z((z + 1) % 4), along_z((z + 3) % 4)
     to_pr, to_pl = device(zl, p_r, q), device(zl, p_l, q)
     to_qr, to_ql = device(zl, p, (q + 1) % 4), device(zl, p, (q + 3) % 4)
     to_qo = device(zl, p, (q + 2) % 4)
@@ -91,7 +103,7 @@
     meta[0] = mrow
 
     barrier = pltpu.get_barrier_semaphore()
-    partners = (to_z, to_pr, to_pl, to_qr, to_ql, to_qo, to_c)
+    partners = (to_zu, to_zd, to_pr, to_pl, to_qr, to_ql, to_qo, to_c)
     for where in partners:
         pl.semaphore_signal(barrier, inc=1, device_id=where, device_id_type=MESH)
     pl.semaphore_wait(barrier, len(partners))
@@ -110,9 +122,6 @@
     def adapter_at(first, size):
         return lambda zl_, p_: src.at[zl_, p_, :, pl.ds(first, size)]
 
-    u_z, u_p1o, u_p1z, u_p2 = gather(up_h.at[0], adapter_at(0, value))
-    d_z, d_p1o, d_p1z, d_p2 = gather(down_h.at[0], adapter_at(value, model))
-    w_z, w_p1o, w_p1z, w_p2 = gather(w_own, lambda zl_, p_: wbuf.at[0, 0, zl_ * 4 + p_])
     m_q = [
         remote(meta.at[0], meta.at[3], to_qr),
         remote(meta.at[0], meta.at[1], to_ql),
@@ -132,9 +141,6 @@
             remote(sel.at[3, :, whole], r2.at[1, :, whole], to_ql),
         ]
         return q1, q2
-
-    u_q1, u_q2 = scatter_q(0, value)
-    d_q1, d_q2 = scatter_q(value, model)
 
     def grads(first, size):
         h = size // 2
@@ -159,25 +165,44 @@
         z = [remote(zs.at[:, whole], t3.at[:, whole], to_z)]
         return q1, q2, p1, p2, z
 
-    gd = grads(value, model)
-    gu = grads(0, value)
-
-    def w_part(dq, zl_):
-        return wbuf.at[0, dq, pl.ds(zl_ * 4, 4)]
-
-    w_q1 = [
-        remote(w_part(0, 0), w_part(3, 0), to_qr),
-        remote(w_part(0, 1), w_part(1, 1), to_ql),
-        remote(w_part(0, 1), w_part(3, 1), to_qr),
-        remote(w_part(0, 0), w_part(1, 0), to_ql),
+    def piece(dq, zl_, p_):
+        return wbuf.at[0, dq, zl_ * 4 + p_]
+
+    def rows_of(ref, first, size):
+        return ref.at[pl.ds(first, size)]
+
+    order = (p, p_l, p_r, p_o)
+    held = [w_own] + [piece(0, zl, k) for k in order[1:]]
+    w_p1 = [remote(w_own, piece(0, zl, p), to_pr), remote(w_own, piece(0, zl, p), to_pl)]
+    w_p2 = [
+        remote(rows_of(held[1], 0, half // 2), rows_of(held[1], 0, half // 2), to_pr),
+        remote(rows_of(held[2], half // 2, half // 2), rows_of(held[2], half // 2, half // 2), to_pl),
     ]
-    w_q2 = [
-        remote(w_part(3, 0), w_part(2, 0), to_qr),
-        remote(w_part(1, 1), w_part(2, 1), to_ql),
-    ]
+    w_q1, w_q2, w_z0, w_z1, w_z2 = [], [], [], [], []
+    for j in range(4):
+        k = order[j]
+        up, down = (to_zu, to_zd) if j % 2 == 0 else (to_zd, to_zu)
+        w_q1.append([
+            remote(held[j], piece(3, zl, k), to_qr),
+            remote(held[j], piece(1, zl, k), to_ql),
+        ])
+        w_z0.append(remote(held[j], piece(0, zl, k), up))
+        w_z1.append([
+            remote(piece(3, zl, k), piece(3, zl, k), up),
+            remote(piece(1, zl, k), piece(1, zl, k), down),
+        ])
+        if j < 2:
+            w_q2.append(remote(piece(3, zl, k), piece(2, zl, k), to_qr))
+        else:
+            w_q2.append(remote(piece(1, zl, k), piece(2, zl, k), to_ql))
+        w_z2.append(remote(piece(2, zl, k), piece(2, zl, k), up))
     w_c = [remote(wbuf.at[0, dq], wbuf.at[1, dq], to_c) for dq in range(4)]
 
-    start(u_z + u_p1o + m_q + d_z + d_p1o + w_z + w_p1o)
+    sent = []
+
+    def go(copies):
+        sent.extend(copies)
+        start(copies)
 
     def columns(first, j, step=STEP):
         return pl.ds(mult(first + j * step, 128), step)
@@ -333,146 +358,184 @@
             return carry
         lax.fori_loop(0, 8, send_out, 0)
 
-    U = (0, value)
-    D = (value, model)
-
-    recv(u_z)
-    start(u_p1z)
-    recv(u_p1o + u_p1z)
-    start(u_p2)
-    recv(d_z)
-    start(d_p1z)
-    recv(m_q)
-    build_selection()
-    lc_up.wait()
-    recv(u_p2)
-    select(*U)
-    start(u_q1)
-    recv(w_z)
-    start(w_p1z)
-    recv(u_q1)
-    add_halves(*U)
-    start(u_q2)
-    recv(d_p1o + d_p1z)
-    start(d_p2)
-    lc_cot.wait()
-    cot[...] = jnp.where(live_mask((rows, value)), cot[...].astype(F32), 0.0).astype(BF16)
-    recv(u_q2)
-    finish_selection(*U)
-
-    back = lax.dot_general(
-        cot[...], fin[:, pl.ds(0, value)], (((1,), (1,)), ((), ())), preferred_element_type=F32
-    )
-    lg[...] = jnp.where(block_mask(), ADAPTER_SCALE * back, 0.0).astype(BF16)
-    lc_tok.wait()
-
-    def down_part(j, step):
+    def adapter_chain(own, first, size):
+        z1, p1o, p1z, p2 = gather(own, adapter_at(first, size))
+        q1, q2 = scatter_q(first, size)
+        go(z1 + p1o)
+        yield
+        recv(z1)
+        go(p1z)
+        yield
+        recv(p1o + p1z)
+        go(p2)
+        yield
+        recv(p2)
+        select(first, size)
+        go(q1)
+        yield
+        recv(q1)
+        add_halves(first, size)
+        go(q2)
+        yield
+        recv(q2)
+        finish_selection(first, size)
+        yield
+
+    def gradient_chain(first, size, make):
+        q1, q2, p1, p2, z1 = grads(first, size)
+        make()
+        go(q1)
+        yield
+        recv(q1)
+        go(q2)
+        yield
+        recv(q2)
+        build_table(first, size)
+        go(p1)
+        yield
+        recv(p1)
+        add_table(first, size)
+        go(p2)
+        yield
+        recv(p2)
+        send_table(first, size)
+        go(z1)
+        yield
+        recv(z1)
+        finish_table(first, size)
+        yield
+
+    def weight_chain():
+        go(w_p1)
+        yield
+        go(w_q1[0] + [w_z0[0]])
+        yield
+        recv([w_p1[0]])
+        go([w_p2[0]] + w_q1[1] + [w_z0[1]])
+        yield
+        recv([w_p1[1]])
+        go([w_p2[1]] + w_q1[2] + [w_z0[2]])
+        yield
+        recv(w_p2)
+        go(w_q1[3] + [w_z0[3]])
+        yield
+        for j in range(4):
+            recv(w_q1[j])
+            go(w_z1[j] + [w_q2[j]])
+            yield
+        for j in (0, 2):
+            recv(w_q2[j : j + 2])
+            go(w_z2[j : j + 2])
+            yield
+
+    def core_chain():
+        lc_w.wait()
+        recv(w_z0)
+        go([w_c[0]])
+        yield
+        for pair in w_z1:
+            recv(pair)
+        go([w_c[1], w_c[3]])
+        yield
+        recv(w_z2)
+        go([w_c[2]])
+        yield
+
+    def batch_chain():
+        t = 0
+        for g, dq in ((0, 0), (0, 1), (0, 3), (1, 0), (1, 1), (1, 3), (0, 2), (1, 2)):
+            if g == 1:
+                recv([w_c[dq]])
+            batch(g, dq, t, t >= 2)
+            t += 1
+            yield
+
+    def mask_chain():
+        lc_cot.wait()
+        cot[...] = jnp.where(live_mask((rows, value)), cot[...].astype(F32), 0.0).astype(BF16)
+        lc_up.wait()
+        lc_down.wait()
+        yield
+
+    def meta_chain():
+        go(m_q)
+        yield
+        recv(m_q)
+        build_selection()
+        yield
+
+    def low_gradient_chain():
+        back = lax.dot_general(
+            cot[...], fin[:, pl.ds(0, value)], (((1,), (1,)), ((), ())), preferred_element_type=F32
+        )
+        lg[...] = jnp.where(block_mask(), ADAPTER_SCALE * back, 0.0).astype(BF16)
+        lc_tok.wait()
+        yield
+
+    def down_parts(first, size):
+        def make():
+            def down_part(j, step):
+                got = lax.dot_general(
+                    lg[...], tok[:, columns(first - value, j, step)], (((0,), (0,)), ((), ())),
+                    preferred_element_type=F32,
+                )
+                part[0, :, columns(first, j, step)] = got.astype(BF16)
+            loop(size, down_part)
+        return make
+
+    def low_chain():
+        def low_part(j, total):
+            return total + lax.dot_general(
+                tok[:, columns(0, j)], fin[:, columns(value, j)], (((1,), (1,)), ((), ())),
+                preferred_element_type=F32,
+            )
+        total = lax.fori_loop(0, model // STEP, low_part, jnp.zeros((rows, picks), F32))
+        low[...] = jnp.where(block_mask(), total, 0.0).astype(BF16)
+        yield
+        acc[...] = ADAPTER_SCALE * jnp.dot(
+            low[...], fin[:, pl.ds(0, value)], preferred_element_type=F32
+        )
+        yield
+
+    def up_part():
         got = lax.dot_general(
-            lg[...], tok[:, columns(0, j, step)], (((0,), (0,)), ((), ())),
-            preferred_element_type=F32,
+            low[...], cot[...], (((0,), (0,)), ((), ())), preferred_element_type=F32
         )
-        part[0, :, columns(value, j, step)] = got.astype(BF16)
-    loop(model, down_part)
-    start(gd[0])
-
-    lc_down.wait()
-    recv(d_p2)
-    select(*D)
-    start(d_q1)
-    recv(w_p1o + w_p1z)
-    start(w_p2)
-    lc_w.wait()
-    recv(w_p2)
-    start(w_q1)
-    start([w_c[0]])
-    recv(gd[0])
-    start(gd[1])
-    recv(d_q1)
-    add_halves(*D)
-    start(d_q2)
-    recv(gd[1])
-    build_table(*D)
-    start(gd[2])
-    recv(d_q2)
-    finish_selection(*D)
-
-    def low_part(j, total):
-        return total + lax.dot_general(
-            tok[:, columns(0, j)], fin[:, columns(value, j)], (((1,), (1,)), ((), ())),
-            preferred_element_type=F32,
+        part[0, :, pl.ds(0, value)] = (ADAPTER_SCALE * got).astype(BF16)
+
+    chains = {
+        "U": adapter_chain(up_h.at[0], 0, value),
+        "GU": gradient_chain(0, value, up_part),
+        "W": weight_chain(),
+        "C": core_chain(),
+        "B": batch_chain(),
+        "M": mask_chain(),
+        "S": meta_chain(),
+        "LG": low_gradient_chain(),
+        "L": low_chain(),
+    }
+    size = model // PARTS
+    for k in range(PARTS):
+        own = down_h.at[0, :, pl.ds(k * size, size)]
+        chains["D%d" % k] = adapter_chain(own, value + k * size, size)
+        chains["G%d" % k] = gradient_chain(
+            value + k * size, size, down_parts(value + k * size, size)
         )
-    total = lax.fori_loop(0, model // STEP, low_part, jnp.zeros((rows, picks), F32))
-    low[...] = jnp.where(block_mask(), total, 0.0).astype(BF16)
-    up_part = lax.dot_general(
-        low[...], cot[...], (((0,), (0,)), ((), ())), preferred_element_type=F32
-    )
-    part[0, :, pl.ds(0, value)] = (ADAPTER_SCALE * up_part).astype(BF16)
-    start(gu[0])
-    acc[...] = ADAPTER_SCALE * jnp.dot(
-        low[...], fin[:, pl.ds(0, value)], preferred_element_type=F32
-    )
-    recv(gd[2])
-    add_table(*D)
-    start(gd[3])
-    recv(gu[0])
-    start(gu[1])
-    recv([w_c[0]])
-
-    def first_batches(i, carry):
-        batch(i, 0, i, False)
-        return carry
-    lax.fori_loop(0, 2, first_batches, 0)
-    recv(gd[3])
-    send_table(*D)
-    start(gd[4])
-    recv(gu[1])
-    build_table(*U)
-    start(gu[2])
-    recv([w_q1[0], w_q1[1]])
-    start(w_q2)
-    recv(gu[2])
-    add_table(*U)
-    start(gu[3])
-    recv([w_q1[2], w_q1[3]])
-    start([w_c[1], w_c[3]])
-    recv(gd[4])
-    finish_table(*D)
-    o_gd = pltpu.make_async_copy(gout.at[:, pl.ds(value, model)], gd_h.at[0], ls.at[5])
-    o_gd.start()
-    recv(gu[3])
-    send_table(*U)
-    start(gu[4])
-    recv([w_c[1], w_c[3]])
-
-    def middle_batches(i, carry):
-        batch(i // 2, 1 + 2 * (i % 2), i + 2, True)
-        return carry
-    lax.fori_loop(0, 4, middle_batches, 0)
-    recv(gu[4])
-    finish_table(*U)
-    o_gu = pltpu.make_async_copy(gout.at[:, pl.ds(0, value)], gu_h.at[0], ls.at[6])
-    o_gu.start()
-    recv(w_q2)
-    start([w_c[2]])
-    recv([w_c[2]])
-
-    def last_batches(i, carry):
-        batch(i, 2, i + 6, True)
-        return carry
-    lax.fori_loop(0, 2, last_batches, 0)
+    for name in " ".join(ORDER).split():
+        next(chains[name])
+
     outb[...] = jnp.where(live_mask((rows, value)), acc[...], 0.0).astype(BF16)
-    o_out = pltpu.make_async_copy(outb, out_h, ls.at[7])
-    o_out.start()
-
-    sent = u_z + u_p1o + u_p1z + u_p2 + d_z + d_p1o + d_p1z + d_p2 + w_z + w_p1o + w_p1z + w_p2
-    sent = sent + m_q + u_q1 + u_q2 + d_q1 + d_q2 + w_q1 + w_q2 + w_c
-    for group in gd + gu:
-        sent = sent + group
+    outs = [
+        pltpu.make_async_copy(outb, out_h, ls.at[5]),
+        pltpu.make_async_copy(gout.at[:, pl.ds(value, model)], gd_h.at[0], ls.at[6]),
+        pltpu.make_async_copy(gout.at[:, pl.ds(0, value)], gu_h.at[0], ls.at[7]),
+    ]
+    start(outs)
+
     for copy in sent:
         copy.wait_send()
-    o_gd.wait()
-    o_gu.wait()
-    o_out.wait()
+    for copy in outs:
+        copy.wait()
     for slot in range(2):
         for i in range(8):
             pltpu.make_async_copy(
@@ -480,6 +543,24 @@
                 tg_h.at[:, pl.ds(i * half, half)],
                 ts.at[slot, i],
             ).wait()
+
+
+COPY_PARTS = 8
+
+
+def copy_out(*refs):
+    sources, targets, sems = refs[:4], refs[4:8], refs[8]
+    rows = sources[1].shape[0] // COPY_PARTS
+    jobs = [(1, pl.ds(i * rows, rows)) for i in range(COPY_PARTS)]
+    jobs = jobs + [(i, pl.ds(0, sources[i].shape[0])) for i in (0, 2, 3)]
+    copies = [
+        pltpu.make_async_copy(sources[i].at[part], targets[i].at[part], sems.at[n])
+        for n, (i, part) in enumerate(jobs)
+    ]
+    for copy in copies:
+        copy.start()
+    for copy in copies:
+        copy.wait()
 
 
 def on_device(
@@ -503,16 +584,17 @@
     smem = pl.BlockSpec(memory_space=pltpu.SMEM)
     vmem = pl.BlockSpec(memory_space=pltpu.VMEM)
     flops = 4 * rows * model * value
-    return pl.pallas_call(
+    shapes = (
+        jax.ShapeDtypeStruct((rows, value), BF16),
+        jax.ShapeDtypeStruct((rows, model), BF16),
+        jax.ShapeDtypeStruct((1, rank, model), BF16),
+        jax.ShapeDtypeStruct((1, rank, value), BF16),
+    )
+    results = pl.pallas_call(
         kernel,
-        out_shape=(
-            jax.ShapeDtypeStruct((rows, value), BF16),
-            jax.ShapeDtypeStruct((rows, model), BF16),
-            jax.ShapeDtypeStruct((1, rank, model), BF16),
-            jax.ShapeDtypeStruct((1, rank, value), BF16),
-        ),
+        out_shape=tuple(pltpu.VMEM(r.shape, r.dtype) for r in shapes),
         in_specs=[hbm] * 5 + [smem, smem, vmem],
-        out_specs=(hbm, hbm, hbm, hbm),
+        out_specs=(vmem,) * 4,
         scratch_shapes=[
             pltpu.VMEM((rows, model), BF16),
             pltpu.VMEM((rows, value), BF16),
@@ -544,7 +626,7 @@
             pltpu.SemaphoreType.DMA((NSEM,)),
         ],
         compiler_params=pltpu.CompilerParams(
-            collective_id=0, has_side_effects=True, vmem_limit_bytes=58 * 2**20
+            collective_id=0, has_side_effects=True, vmem_limit_bytes=56 * 2**20
         ),
         cost_estimate=pl.CostEstimate(
             flops=flops, bytes_accessed=4 * rows * model, transcendentals=0
@@ -559,6 +641,14 @@
         block_live_rows,
         tenant_owner_slot.reshape(1, -1),
     )
+    return pl.pallas_call(
+        copy_out,
+        out_shape=shapes,
+        in_specs=[hbm] * 4,
+        compiler_params=pltpu.CompilerParams(vmem_limit_bytes=4 * 2**20),
+        out_specs=(hbm,) * 4,
+        scratch_shapes=[pltpu.SemaphoreType.DMA((COPY_PARTS + 3,))],
+    )(*results)
 
 
 def solution(mesh):

time: 153 us -> 102 us (0.67)
  Pallas kernels: 142 us -> 100 us
  local copies, waits for them, and re-layouts: 9.63 us -> 0 us
    pallas_call x1 -> x2, Pallas kernels: 142 us -> 100 us  [the longest x1 97.2 us: on_device(): pl.pallas_call(kernel, out_shape=tuple((pltpu.VMEM(r.shape, r.dtype) for...]
    unnamed x8 -> x0, local copies, waits for them, and re-layouts: 9.63 us -> none
where the time goes in v2:
time: 102 us; the launch traced here: 101 us
  Pallas kernels  100 us (98%)
    pallas_call x1, Pallas kernels, on_device(): pl.pallas_call(kernel, out_shape=tuple((pltpu.VMEM(r.shape, r.dtype) for...  97.2 us
    pallas_call x1, Pallas kernels, on_device(): pl.pallas_call(copy_out, out_shape=shapes, in_specs=[hbm] * 4, compiler_p...  3.07 us

profile of v2, /device:TPU:0, one launch (start us, length us, event | category | flops | bytes accessed | tf_op | source)
XLA Modules:
  0.0 100.9 jit_solution(12682397184312511608)
XLA Ops:
  0.6 97.2 %shard_map.111 = (bf16[384,1024]{1,0:T(8,128)(2,1)S(1)}, bf16[384,8192]{1,0:T(8,128)(2,1)S(1)}, bf16[1,16,8192]{2,1,0:T(8,128)(2,1)S(1)}, bf16[1,16,1024]{2,1,0:T(8,128)(2,1)S(1)}) custom-call(bf16[384,8192]{1,0:T(8,128)(2,1)} %tok_h.1, bf16[384,1024]{1,0:T(8,128)(2,1)} %cot_h.1, bf16[256,1024]{1,0:T(8,128)(2,1)} %w_h.1, bf16[1,16,8192]{2,1,0:T(8,128)(2,1)} %down_h.1, ...), custom_call_target="tpu_custom_call" | custom-call | flops 12884901888 | bytes 12582912 | tf_op jit(solution)/shard_map/pallas_call | solution.py:593
  97.9 3.1 %shard_map.112 = (bf16[384,1024]{1,0:T(8,128)(2,1)}, bf16[384,8192]{1,0:T(8,128)(2,1)}, bf16[1,16,8192]{2,1,0:T(8,128)(2,1)}, bf16[1,16,1024]{2,1,0:T(8,128)(2,1)}) custom-call(bf16[384,1024]{1,0:T(8,128)(2,1)S(1)} %get-tuple-element.8.refs_0_, bf16[384,8192]{1,0:T(8,128)(2,1)S(1)} %get-tuple-element.9.refs_1_, ...), custom_call_target="tpu_custom_call" | custom-call | tf_op jit(solution)/shard_map/pallas_call | solution.py:644

commit v3 on v2

--- a/solution.py
+++ b/solution.py
@@ -11,11 +11,12 @@
 BF16 = jnp.bfloat16
 STEP = 1024
 NSEM = 128
+NTILE = 256
 PARTS = 2
 ORDER = (
-    "U S D0 D1", "W W M U", "D0 W D1 U", "W D0 D1 S", "U W W D0", "D1 U C W",
-    "W W D0 D1", "U LG G0 G1", "D0 D1 L G0", "GU L C B", "W W B G1", "B G0 GU G1",
-    "B G0 GU G1", "B C B G0", "GU B G1 GU", "B G0 G1 GU",
+    "U S D0 D1", "W W M S", "U D0 W W", "D1 U LG D0", "G0 G1 W W", "W W D1 D0",
+    "C F G0 F", "G1 W W D1", "D0 G0 W G1", "C F D1 F", "D0 F G0 G1", "F C F D1",
+    "L G0 GU G1", "R R G0 GU", "R G1 R R", "GU R R F", "R",
 )
 
 
@@ -26,8 +27,8 @@
 def kernel(
     tok_h, cot_h, w_h, down_h, up_h, ids_s, live_s, owner_v,
     out_h, tg_h, gd_h, gu_h,
-    tok, cot, wbuf, src, sel, r1, r2, fin, part, tab, t1, t2, t3, zs, gout,
-    acc, xb, db, tgb, outb, meta, smat, lg, low, ls, ts, ss, rs,
+    tok, cot, wbuf, src, sel, r1, r2, fin, part, tab, t1, t2, t3, zs, ru, tu,
+    acc, xb, meta, smat, lg, low, ls, ss, rs,
 ):
     rows, model = tok_h.shape
     value = cot_h.shape[1]
@@ -103,7 +104,11 @@
     meta[0] = mrow
 
     barrier = pltpu.get_barrier_semaphore()
-    partners = (to_zu, to_zd, to_pr, to_pl, to_qr, to_ql, to_qo, to_c)
+    near = [(a, b) for a in range(2) for b in range(4) if (a, b) != (0, 0)]
+    to_near = [device((zl + a) % 2, (p + b) % 4, q) for a, b in near]
+    to_q = [to_qr, to_qo, to_ql]
+    to_other_z = along_z((z + 3 + 2 * zl) % 4)
+    partners = to_near + to_q + [to_other_z, to_c]
     for where in partners:
         pl.semaphore_signal(barrier, inc=1, device_id=where, device_id_type=MESH)
     pl.semaphore_wait(barrier, len(partners))
@@ -289,7 +294,8 @@
     def finish_table(first, size):
         def one(j, step):
             cols = columns(first, j, step)
-            gout[:, cols] = (sum_three(zl, cols) + t3[:, cols].astype(F32)).astype(BF16)
+            total = sum_three(zl, cols) + t3[:, cols].astype(F32)
+            gd_h[0, :, columns(first - value, j, step)] = total.astype(BF16)
         loop(size, one)
 
     def live_mask(shape):
@@ -304,59 +310,37 @@
         k = lax.broadcasted_iota(jnp.int32, (rows, picks), 1)
         return jnp.logical_and(r // block == k // rank, live_mask((rows, picks)))
 
-    def batch(g, dq, t, wait):
+    def place(g, dq, i):
         spg = sp + g * (sq - sp)
         sqg = sq + g * (sp - sq)
         qg = q + g * (p - q)
         hg = c + g * (1 - 2 * c)
-        slot = t % 2
-
-        def place(i):
-            f = (i // 4) * 16 + (i % 4) * spg + ((qg + dq) % 4) * sqg
-            return mult(f * (2 * half) + hg * half, half)
-
-        def take(i, carry):
-            at = pl.ds(mult(i * half, half), half)
-            xb[:, at] = tok[:, pl.ds(place(i), half)]
-            db[:, at] = fin[:, pl.ds(mult(value + place(i), half), half)]
-            return carry
-        lax.fori_loop(0, 8, take, 0)
-
-        def forward(n, carry):
-            cols = pl.ds(mult(n * 256, 256), 256)
-            w = wbuf[g, dq, :, :, cols].reshape(8 * half, 256)
-            acc[:, cols] += jnp.dot(xb[...], w, preferred_element_type=F32)
-            return carry
-        lax.fori_loop(0, value // 256, forward, 0)
-
-        def out_copy(i):
-            return pltpu.make_async_copy(
-                tgb.at[slot, :, pl.ds(mult(i * half, half), half)],
-                tg_h.at[:, pl.ds(place(i), half)],
-                ts.at[slot, i],
-            )
-
-        if wait:
-            def settle(i, carry):
-                out_copy(i).wait()
-                return carry
-            lax.fori_loop(0, 8, settle, 0)
-
-        def backward(m, carry):
-            w = wbuf[g, dq, pl.ds(m * 2, 2), :, :].reshape(2 * half, value)
-            at = pl.ds(mult(m * 2 * half, 2 * half), 2 * half)
+        f = (i // 4) * 16 + (i % 4) * spg + ((qg + dq) % 4) * sqg
+        return mult(f * (2 * half) + hg * half, half)
+
+    def forward(g, dq, first):
+        for i in range(8):
+            xb[:, i * half : (i + 1) * half] = tok[:, pl.ds(place(g, dq, i), half)]
+        for n in range(value // NTILE):
+            cols = pl.ds(n * NTILE, NTILE)
+            w = wbuf[g, dq, :, :, cols].reshape(8 * half, NTILE)
+            got = jnp.dot(xb[...], w, preferred_element_type=F32)
+            acc[:, cols] = got if first else acc[:, cols] + got
+
+    def backward(g, dq):
+        for m in range(4):
+            w = wbuf[g, dq, 2 * m : 2 * m + 2, :, :].reshape(2 * half, value)
+            here = [place(g, dq, 2 * m + i) for i in range(2)]
+            maps = [fin[:, pl.ds(mult(value + at, half), half)] for at in here]
             got = lax.dot_general(
                 cot[...], w, (((1,), (1,)), ((), ())), preferred_element_type=F32
             )
-            got = got + jnp.dot(lg[...], db[:, at], preferred_element_type=F32)
-            tgb[slot, :, at] = got.astype(BF16)
-            return carry
-        lax.fori_loop(0, 4, backward, 0)
-
-        def send_out(i, carry):
-            out_copy(i).start()
-            return carry
-        lax.fori_loop(0, 8, send_out, 0)
+            got = got + jnp.dot(
+                lg[...], jnp.concatenate(maps, axis=1), preferred_element_type=F32
+            )
+            got = got.astype(BF16)
+            for i in range(2):
+                tg_h[:, pl.ds(here[i], half)] = got[:, i * half : (i + 1) * half]
 
     def adapter_chain(own, first, size):
         z1, p1o, p1z, p2 = gather(own, adapter_at(first, size))
@@ -379,6 +363,50 @@
         yield
         recv(q2)
         finish_selection(first, size)
+        yield
+
+    def up_chain():
+        at = pl.ds(0, value)
+        spread = [
+            remote(up_h.at[0], src.at[zl, p, :, at], where) for where in to_near
+        ]
+        go(spread)
+        yield
+        recv(spread)
+        select(0, value)
+        deliver = [
+            remote(sel.at[i + 1, :, at], ru.at[i], to_q[i]) for i in range(3)
+        ]
+        go(deliver)
+        yield
+        recv(deliver)
+        fin[:, at] = sel[0, :, at] + ru[0] + ru[1] + ru[2]
+        yield
+
+    def up_gradient_chain():
+        at = pl.ds(0, value)
+        got = lax.dot_general(
+            low[...], cot[...], (((0,), (0,)), ((), ())), preferred_element_type=F32
+        )
+        part[0, :, at] = (ADAPTER_SCALE * got).astype(BF16)
+        spread = [
+            remote(part.at[0, :, at], part.at[3 - i, :, at], to_q[i]) for i in range(3)
+        ]
+        go(spread)
+        yield
+        recv(spread)
+        build_table(0, value)
+        collect = [
+            remote(tab.at[(zl + a) % 2, (p + b) % 4, :, at], tu.at[i], to_near[i])
+            for i, (a, b) in enumerate(near)
+        ]
+        go(collect)
+        yield
+        recv(collect)
+        total = tab[zl, p, :, at].astype(F32)
+        for i in range(7):
+            total = total + tu[i].astype(F32)
+        gu_h[0] = total.astype(BF16)
         yield
 
     def gradient_chain(first, size, make):
@@ -441,17 +469,23 @@
         go([w_c[2]])
         yield
 
-    def batch_chain():
-        t = 0
-        for g, dq in ((0, 0), (0, 1), (0, 3), (1, 0), (1, 1), (1, 3), (0, 2), (1, 2)):
+    batches = ((0, 0), (1, 0), (0, 1), (0, 3), (1, 1), (1, 3), (0, 2), (1, 2))
+
+    def forward_chain():
+        for n, (g, dq) in enumerate(batches):
             if g == 1:
                 recv([w_c[dq]])
-            batch(g, dq, t, t >= 2)
-            t += 1
+            forward(g, dq, n == 0)
+            yield
+
+    def backward_chain():
+        for g, dq in batches:
+            backward(g, dq)
             yield
 
     def mask_chain():
         lc_cot.wait()
+        lc_tok.wait()
         cot[...] = jnp.where(live_mask((rows, value)), cot[...].astype(F32), 0.0).astype(BF16)
         lc_up.wait()
         lc_down.wait()
@@ -469,7 +503,6 @@
             cot[...], fin[:, pl.ds(0, value)], (((1,), (1,)), ((), ())), preferred_element_type=F32
         )
         lg[...] = jnp.where(block_mask(), ADAPTER_SCALE * back, 0.0).astype(BF16)
-        lc_tok.wait()
         yield
 
     def down_parts(first, size):
@@ -492,23 +525,14 @@
         total = lax.fori_loop(0, model // STEP, low_part, jnp.zeros((rows, picks), F32))
         low[...] = jnp.where(block_mask(), total, 0.0).astype(BF16)
         yield
-        acc[...] = ADAPTER_SCALE * jnp.dot(
-            low[...], fin[:, pl.ds(0, value)], preferred_element_type=F32
-        )
-        yield
-
-    def up_part():
-        got = lax.dot_general(
-            low[...], cot[...], (((0,), (0,)), ((), ())), preferred_element_type=F32
-        )
-        part[0, :, pl.ds(0, value)] = (ADAPTER_SCALE * got).astype(BF16)
 
     chains = {
-        "U": adapter_chain(up_h.at[0], 0, value),
-        "GU": gradient_chain(0, value, up_part),
+        "U": up_chain(),
+        "GU": up_gradient_chain(),
         "W": weight_chain(),
         "C": core_chain(),
-        "B": batch_chain(),
+        "F": forward_chain(),
+        "R": backward_chain(),
         "M": mask_chain(),
         "S": meta_chain(),
         "LG": low_gradient_chain(),
@@ -524,25 +548,15 @@
     for name in " ".join(ORDER).split():
         next(chains[name])
 
-    outb[...] = jnp.where(live_mask((rows, value)), acc[...], 0.0).astype(BF16)
-    outs = [
-        pltpu.make_async_copy(outb, out_h, ls.at[5]),
-        pltpu.make_async_copy(gout.at[:, pl.ds(value, model)], gd_h.at[0], ls.at[6]),
-        pltpu.make_async_copy(gout.at[:, pl.ds(0, value)], gu_h.at[0], ls.at[7]),
-    ]
-    start(outs)
+    for n in range(value // NTILE):
+        cols = pl.ds(n * NTILE, NTILE)
+        total = acc[:, cols] + ADAPTER_SCALE * jnp.dot(
+            low[...], fin[:, cols], preferred_element_type=F32
+        )
+        out_h[:, cols] = jnp.where(live_mask((rows, NTILE)), total, 0.0).astype(BF16)
 
     for copy in sent:
         copy.wait_send()
-    for copy in outs:
-        copy.wait()
-    for slot in range(2):
-        for i in range(8):
-            pltpu.make_async_copy(
-                tgb.at[slot, :, pl.ds(i * half, half)],
-                tg_h.at[:, pl.ds(i * half, half)],
-                ts.at[slot, i],
-            ).wait()
 
 
 COPY_PARTS = 8
@@ -610,18 +624,15 @@
             pltpu.VMEM((2, 2, rank, width), BF16),
             pltpu.VMEM((rank, width), BF16),
             pltpu.VMEM((rank, width), BF16),
-            pltpu.VMEM((rank, width), BF16),
+            pltpu.VMEM((3, picks, value), BF16),
+            pltpu.VMEM((7, rank, value), BF16),
             pltpu.VMEM((rows, value), F32),
             pltpu.VMEM((rows, 8 * half), BF16),
-            pltpu.VMEM((picks, 8 * half), BF16),
-            pltpu.VMEM((2, rows, 8 * half), BF16),
-            pltpu.VMEM((rows, value), BF16),
             pltpu.VMEM((4, 8, 128), F32),
             pltpu.VMEM((4 * picks, 8 * rank), BF16),
             pltpu.VMEM((rows, picks), BF16),
             pltpu.VMEM((rows, picks), BF16),
             pltpu.SemaphoreType.DMA((8,)),
-            pltpu.SemaphoreType.DMA((2, 8)),
             pltpu.SemaphoreType.DMA((NSEM,)),
             pltpu.SemaphoreType.DMA((NSEM,)),
         ],

time: 102 us -> 97.6 us (0.957)
  Pallas kernels: 100 us -> 96.7 us
    pallas_call x1, Pallas kernels: 97.2 us -> 93.7 us  [on_device(): pl.pallas_call(kernel, out_shape=tuple((pltpu.VMEM(r.shape, r.dtype) for...]
where the time goes in v3:
time: 97.6 us; the launch traced here: 97.5 us
  Pallas kernels  96.7 us (99%)
    pallas_call x1, Pallas kernels, on_device(): pl.pallas_call(kernel, out_shape=tuple((pltpu.VMEM(r.shape, r.dtype) for...  93.7 us
    pallas_call x1, Pallas kernels, on_device(): pl.pallas_call(copy_out, out_shape=shapes, in_specs=[hbm] * 4, compiler_p...  3.07 us

profile of v3, /device:TPU:0, one launch (start us, length us, event | category | flops | bytes accessed | tf_op | source)
XLA Modules:
  0.0 97.5 jit_solution(9435365188376377732)
XLA Ops:
  0.6 93.7 %shard_map.111 = (bf16[384,1024]{1,0:T(8,128)(2,1)S(1)}, bf16[384,8192]{1,0:T(8,128)(2,1)S(1)}, bf16[1,16,8192]{2,1,0:T(8,128)(2,1)S(1)}, bf16[1,16,1024]{2,1,0:T(8,128)(2,1)S(1)}) custom-call(bf16[384,8192]{1,0:T(8,128)(2,1)} %tok_h.1, bf16[384,1024]{1,0:T(8,128)(2,1)} %cot_h.1, bf16[256,1024]{1,0:T(8,128)(2,1)} %w_h.1, bf16[1,16,8192]{2,1,0:T(8,128)(2,1)} %down_h.1, ...), custom_call_target="tpu_custom_call" | custom-call | flops 12884901888 | bytes 12582912 | tf_op jit(solution)/shard_map/pallas_call | solution.py:607
  94.3 3.1 %shard_map.112 = (bf16[384,1024]{1,0:T(8,128)(2,1)}, bf16[384,8192]{1,0:T(8,128)(2,1)}, bf16[1,16,8192]{2,1,0:T(8,128)(2,1)}, bf16[1,16,1024]{2,1,0:T(8,128)(2,1)}) custom-call(bf16[384,1024]{1,0:T(8,128)(2,1)S(1)} %get-tuple-element.8.refs_0_, bf16[384,8192]{1,0:T(8,128)(2,1)S(1)} %get-tuple-element.9.refs_1_, ...), custom_call_target="tpu_custom_call" | custom-call | tf_op jit(solution)/shard_map/pallas_call | solution.py:655

commit v4 on v3

--- a/solution.py
+++ b/solution.py
@@ -11,12 +11,12 @@
 BF16 = jnp.bfloat16
 STEP = 1024
 NSEM = 128
-NTILE = 256
+NTILE = 512
 PARTS = 2
 ORDER = (
-    "U S D0 D1", "W W M S", "U D0 W W", "D1 U LG D0", "G0 G1 W W", "W W D1 D0",
-    "C F G0 F", "G1 W W D1", "D0 G0 W G1", "C F D1 F", "D0 F G0 G1", "F C F D1",
-    "L G0 GU G1", "R R G0 GU", "R G1 R R", "GU R R F", "R",
+    "U S W D0", "W M S U", "W D1 W D1", "U D0 W LG", "G1 W G0 D1", "C D0 W F",
+    "F W W G1", "G0 D0 D1 W", "G1 G0 C D0", "W F F D1", "F F D0 G1", "G0 C F D1",
+    "L GU G1 F", "R R G0 R", "R G1 GU R", "R R R GU", "G0",
 )
 
 

time: 97.6 us -> 94.1 us (0.964)
  Pallas kernels: 96.7 us -> 93 us
    pallas_call x1, Pallas kernels: 93.7 us -> 89.9 us  [on_device(): pl.pallas_call(kernel, out_shape=tuple((pltpu.VMEM(r.shape, r.dtype) for...]
where the time goes in v4:
time: 94.1 us; the launch traced here: 93.8 us
  Pallas kernels  93 us (99%)
    pallas_call x1, Pallas kernels, on_device(): pl.pallas_call(kernel, out_shape=tuple((pltpu.VMEM(r.shape, r.dtype) for...  89.9 us
    pallas_call x1, Pallas kernels, on_device(): pl.pallas_call(copy_out, out_shape=shapes, in_specs=[hbm] * 4, compiler_p...  3.07 us

profile of v4, /device:TPU:0, one launch (start us, length us, event | category | flops | bytes accessed | tf_op | source)
XLA Modules:
  0.0 93.8 jit_solution(9386909333938282329)
XLA Ops:
  0.6 89.9 %shard_map.111 = (bf16[384,1024]{1,0:T(8,128)(2,1)S(1)}, bf16[384,8192]{1,0:T(8,128)(2,1)S(1)}, bf16[1,16,8192]{2,1,0:T(8,128)(2,1)S(1)}, bf16[1,16,1024]{2,1,0:T(8,128)(2,1)S(1)}) custom-call(bf16[384,8192]{1,0:T(8,128)(2,1)} %tok_h.1, bf16[384,1024]{1,0:T(8,128)(2,1)} %cot_h.1, bf16[256,1024]{1,0:T(8,128)(2,1)} %w_h.1, bf16[1,16,8192]{2,1,0:T(8,128)(2,1)} %down_h.1, ...), custom_call_target="tpu_custom_call" | custom-call | flops 12884901888 | bytes 12582912 | tf_op jit(solution)/shard_map/pallas_call | solution.py:607
  90.6 3.1 %shard_map.112 = (bf16[384,1024]{1,0:T(8,128)(2,1)}, bf16[384,8192]{1,0:T(8,128)(2,1)}, bf16[1,16,8192]{2,1,0:T(8,128)(2,1)}, bf16[1,16,1024]{2,1,0:T(8,128)(2,1)}) custom-call(bf16[384,1024]{1,0:T(8,128)(2,1)S(1)} %get-tuple-element.8.refs_0_, bf16[384,8192]{1,0:T(8,128)(2,1)S(1)} %get-tuple-element.9.refs_1_, ...), custom_call_target="tpu_custom_call" | custom-call | tf_op jit(solution)/shard_map/pallas_call | solution.py:655
